TPU v7x, 32 devices: a whole 2x2x4 slice. The times are simulated.
32 devices in a mesh: group: 1, shard: 32 (over z, y, x, core).
Axes of the slice: x: 2, y: 2, z: 4, core: 2. Of those that a mesh axis runs over, the one named last changes fastest.
Arguments:
- activations: bfloat16 [64, 256, 4096], P(('group', 'shard')), may hold values from -6 to 6
- out_grads: bfloat16 [64, 256, 1024], P(('group', 'shard')), may hold values from -6 to 6
- value_weight: bfloat16 [4096, 1024], P('shard'), may hold values from -0.09375 to 0.09375
- basis_in: bfloat16 [4096, 64], replicated, may hold values from -0.09375 to 0.09375
- basis_out: bfloat16 [1024, 64], replicated, may hold values from -0.1875 to 0.1875
- doc_lengths: int32 [64], P(('group', 'shard')), may hold values from 1 to 256, 12288 in all
- queries: bfloat16 [1024, 4096], P('shard'), may hold values from -0.005859375 to 0.005859375
Outputs:
- input_grad: bfloat16 [64, 256, 4096], P(('group', 'shard'))
- scores: float32 [1024, 64], P('shard', 'group')
All inputs are finite; a program needn't handle non-finite values. No bound on the sum of `doc_lengths` on one device may be relied on, other than what follows from the above.
Results may differ from a plain program's by a relative error of at most 0.0058.
Values may be sent and summed in bfloat16 or wider, within the bound.
A program may use at most 64 MiB of HBM per device.

v0:
```python
import jax
import jax.numpy as jnp
from jax import lax
from jax.sharding import PartitionSpec as P


def per_device(activations, out_grads, value_weight, basis_in, basis_out, doc_lengths, queries):
    docs = activations.shape[0]
    length = activations.shape[1]
    rank = basis_in.shape[1]
    positions = jnp.arange(length, dtype=jnp.int32)
    valid = (positions[None, :] < doc_lengths[:, None]).astype(jnp.float32)
    full = jnp.einsum(
        "dtk,jk->dtj",
        out_grads,
        lax.all_gather(value_weight, "shard", axis=0, tiled=True),
        preferred_element_type=jnp.float32,
    )
    input_grad = (full * valid[:, :, None]).astype(jnp.bfloat16)
    reduced_in = jnp.einsum(
        "dtk,kr->dtr", activations, basis_in, preferred_element_type=jnp.float32
    ).astype(jnp.bfloat16)
    reduced_out = jnp.einsum(
        "dtk,kr->dtr", out_grads, basis_out, preferred_element_type=jnp.float32
    )
    reduced_out = (reduced_out * valid[:, :, None]).astype(jnp.bfloat16)
    projected = jnp.einsum(
        "dti,dto->dio", reduced_in, reduced_out, preferred_element_type=jnp.float32
    )
    projected = projected.astype(jnp.bfloat16).reshape(docs, rank * rank)
    scores = jnp.dot(
        queries,
        lax.all_gather(projected, "shard", axis=0, tiled=True).T,
        preferred_element_type=jnp.float32,
    )
    return (input_grad, scores)


def solution(mesh):
    placed = (
        P(("group", "shard"), None, None),
        P(("group", "shard"), None, None),
        P("shard", None),
        P(),
        P(),
        P(("group", "shard")),
        P("shard", None),
    )
    return jax.shard_map(
        per_device,
        mesh=mesh,
        in_specs=placed,
        out_specs=(P(("group", "shard"), None, None), P("shard", "group")),
        check_vma=False,
    )
```

profile of v0, /device:TPU:0, one launch (start us, length us, event | category | flops | bytes accessed | tf_op | source)
XLA Modules:
  0.0 108.5 jit_solution(3333696319882959822)
XLA Ops:
  7.2 0.0 copy-start
  7.2 0.0 all-gather.3.cloned.1.call-start
  7.2 0.7 all-gather.3.cloned.1.call-update
  7.9 0.7 compare_convert_fusion
  8.6 0.0 copy-done
  8.6 1.3 %fusion.4 = bf16[2,256,64]{1,2,0:T(8,128)(2,1)S(1)} fusion(bf16[2,256,1024]{2,1,0:T(8,128)(2,1)S(1)} %copy-done, bf16[1024,64]{0,1:T(8,128)(2,1)} %param.11, f32[2,256]{1,0:T(2,128)S(1)} %compare_convert_fusion), kind=kOutput, calls=%fused_computation.4 | convolution fusion | flops 67174400 | bytes 1247232 | tf_op jit(solution)/shard_map/dtk,kr->dtr/dot_general | solution.py:23
  10.0 3.8 %fusion.6 = bf16[2,64,64]{2,1,0:T(8,128)(2,1)S(1)} fusion(bf16[2,256,64]{1,2,0:T(8,128)(2,1)S(1)} %fusion.4, bf16[2,256,4096]{2,1,0:T(8,128)(2,1)} %param.7, bf16[4096,64]{0,1:T(8,128)(2,1)} %param.10), kind=kOutput, calls=%fused_computation.7 | convolution fusion | flops 272670720 | bytes 4800512 | tf_op jit(solution)/shard_map/dti,dto->dio/dot_general | solution.py:27
  13.8 0.1 reshape.30
  13.9 45.8 %all-gather = bf16[32,2,4096]{2,1,0:T(2,128)(2,1)S(1)} all-gather(bf16[1,2,4096]{2,1,0:T(2,128)(2,1)S(1)} %reshape.30), channel_id=1, replica_groups=mesh['group'=1,'shard'=32] {'shard'}, dimensions={0}, use_global_device_ids=true | all-gather | bytes 540672 | tf_op jit(solution)/shard_map/all_gather | solution.py:33
  59.7 0.2 reshape.31
  59.9 1.8 %convolution_bitcast_fusion = f32[32,64]{1,0:T(8,128)} fusion(bf16[64,4096]{1,0:T(8,128)(2,1)S(1)} %reshape.31, bf16[32,4096]{1,0:T(8,128)(2,1)} %param.13), kind=kOutput, calls=%fused_computation.8 | convolution fusion | flops 16777216 | bytes 794624 | tf_op jit(solution)/shard_map/dot_general | solution.py:31
  61.8 30.4 %all-gather.3.cloned.1.call-done = bf16[4096,1024]{1,0:T(8,128)(2,1)} async-done(((bf16[128,1024]{1,0:T(8,128)(2,1)}), bf16[4096,1024]{1,0:T(8,128)(2,1)}) %all-gather.3.cloned.1.call-update) | async-done | bytes 8388624 | tf_op jit(solution)/shard_map/all_gather | solution.py:16
  92.2 9.5 %multiply_convert_fusion = bf16[2,256,4096]{2,1,0:T(8,128)(2,1)} fusion(bf16[2,256,1024]{2,1,0:T(8,128)(2,1)S(1)} %copy-done, bf16[4096,1024]{1,0:T(8,128)(2,1)} %all-gather.3.cloned.1.call-done, f32[2,256]{1,0:T(2,128)S(1)} %compare_convert_fusion), kind=kOutput, calls=%fused_computation.2 | convolution fusion | flops 4299161600 | bytes 13633536 | tf_op jit(solution)/shard_map/dtk,jk->dtj/dot_general | solution.py:13
Async XLA Ops:
  7.2 1.5 %copy-start = (bf16[2,256,1024]{2,1,0:T(8,128)(2,1)S(1)}, bf16[2,256,1024]{2,1,0:T(8,128)(2,1)}, u32[]{:S(2)}) copy-start(bf16[2,256,1024]{2,1,0:T(8,128)(2,1)} %param.8) | copy-start | bytes 3145732
  7.2 85.0 %all-gather.3.cloned.1.call-start = ((), (), s32[]{:S(2)}) async-start(), calls=%async_computation | async-start | bytes 8650752 | tf_op jit(solution)/shard_map/all_gather | solution.py:16
Sparse Core Ops, SparseCore 0:
  10.9 81.2 all-gather.2
where the time goes:
time: 109 us
  blocking collectives  45.8 us (42%)
  waiting for transfers between devices  31.1 us (29%)
  matrix products  16.5 us (15%)
  between operations  14 us (13%)
    all_gather x1, blocking collectives, per_device(): lax.all_gather(projected, 'shard', axis=0, tiled=True)  45.8 us
    all_gather x1, waiting for transfers between devices, per_device(): lax.all_gather(value_weight, 'shard', axis=0, tiled=True)  30.4 us
    dot_general x1, matrix products, per_device(): jnp.einsum('dtk,jk->dtj', out_grads, lax.all_gather(value_weight, 'shard'...  9.46 us
    dot_general x1, matrix products, per_device(): jnp.einsum('dti,dto->dio', reduced_in, reduced_out, preferred_element_typ...  3.82 us
  transfers between devices with their start and end apart: 1, of which 1 were waited for; matrix products, arithmetic and copies ran while one was open for 7% of the time, Pallas kernels for 0%

commit v1 on v0

v1 whole, which is shorter than its diff:
```python
import functools

import jax
import jax.numpy as jnp
from jax import lax
from jax.experimental import pallas as pl
from jax.experimental.pallas import tpu as pltpu
from jax.sharding import PartitionSpec as P

LINK_X, LINK_Y, LINK_CORE = 0, 1, 2
PARTS = 3


def kernel(
    dims, wrap, lengths, act_hbm, grads_hbm, own_hbm, basis_in_hbm, basis_out_hbm, queries_hbm,
    out_hbm, scores_ref,
    weight, projected, act, grads, basis_in, basis_out, queries, staged, gram, wide, flat,
    load_sem, recv_sem, along_sem, link_sem, out_sem,
):
    depth, height, width = dims
    chips = depth * height * width
    me = lax.axis_index("shard")
    core = lax.rem(me, 2)
    x = lax.rem(lax.div(me, 2), width)
    y = lax.rem(lax.div(me, 2 * width), height)
    z = lax.div(me, 2 * width * height)
    rows = own_hbm.shape[0]
    half = rows // 2
    docs = lengths.shape[0]
    length = grads.shape[0] // docs
    rank = basis_in.shape[1]
    packed = projected.shape[0] // (2 * chips)
    per_doc = packed // docs
    plane = width > 1
    reach = depth // 2 + 1 if wrap else depth

    def index(at_z, at_y, at_x, at_core):
        return ((at_z * height + at_y) * width + at_x) * 2 + at_core

    def device(shard):
        return {"shard": shard}

    sibling = index(z, y, x, 1 - core)
    beside_x = index(z, y, 1 - x, core) if plane else None
    beside_y = index(z, 1 - y, x, core) if plane else None

    def at(side, far):
        return lax.rem(z + side * far + depth, depth) if wrap else z + side * far

    def exists(side, far):
        if wrap:
            last = depth // 2 if side > 0 else (depth - 1) // 2
            return (far >= (0 if side > 0 else 1)) & (far <= last)
        if side > 0:
            return (far >= 0) & (z + far < depth)
        return (far >= 1) & (z - far >= 0)

    def goes_on(side, far):
        if wrap:
            return far + 1 <= (depth // 2 if side > 0 else (depth - 1) // 2)
        return z > 0 if side > 0 else z < depth - 1

    def place(shard, part):
        if part == 2:
            return projected.at[pl.ds(pl.multiple_of(shard * packed, packed), packed)]
        return weight.at[pl.ds(pl.multiple_of(shard * rows + part * half, half), half)]

    def copy(shard, part, to, send_sem, source=None):
        target = place(shard, part)
        return pltpu.make_async_remote_copy(
            src_ref=target if source is None else source,
            dst_ref=target,
            send_sem=send_sem,
            recv_sem=recv_sem.at[shard * PARTS + part],
            device_id=device(to),
            device_id_type=pl.DeviceIdType.MESH,
        )

    def link(which, part):
        return link_sem.at[which * 2 + (1 if part == 2 else 0)]

    def arrived(shard, part):
        copy(shard, part, sibling, link(LINK_CORE, part)).wait_recv()

    def along(side, far, part):
        return along_sem.at[((0 if side > 0 else 1) * reach + far) * PARTS + part]

    def send_along(side, far, shard, part, source=None):
        @pl.when(goes_on(side, far))
        def _():
            copy(shard, part, index(at(-side, 1), y, x, core), along(side, far, part), source).start()

    def send_x(shard, part, source=None):
        if plane:
            copy(shard, part, beside_x, link(LINK_X, part), source).start()

    def send_y(shard, part, source=None):
        if plane:
            copy(shard, part, beside_y, link(LINK_Y, part), source).start()

    def send_core(shard, part, source=None):
        copy(shard, part, sibling, link(LINK_CORE, part), source).start()

    own = weight.at[pl.ds(pl.multiple_of(me * rows, rows), rows)]
    loads = [
        pltpu.make_async_copy(source, target, load_sem.at[i])
        for i, (source, target) in enumerate(
            [
                (grads_hbm, grads),
                (basis_out_hbm, basis_out),
                (basis_in_hbm, basis_in),
                (act_hbm, act),
                (own_hbm, own),
                (queries_hbm, queries),
            ]
        )
    ]
    for load in loads:
        load.start()

    barrier = pltpu.get_barrier_semaphore()

    def greet(other):
        pl.semaphore_signal(barrier, inc=1, device_id=device(other), device_id_type=pl.DeviceIdType.MESH)

    greet(sibling)
    if plane:
        greet(beside_x)
        greet(beside_y)
    partners = 3 if plane else 1
    if wrap:
        greet(index(at(1, 1), y, x, core))
        greet(index(at(-1, 1), y, x, core))
        pl.semaphore_wait(barrier, partners + 2)
    else:
        @pl.when(z + 1 < depth)
        def _():
            greet(index(z + 1, y, x, core))

        @pl.when(z > 0)
        def _():
            greet(index(z - 1, y, x, core))

        pl.semaphore_wait(
            barrier, partners + jnp.where(z + 1 < depth, 1, 0) + jnp.where(z > 0, 1, 0)
        )

    for part in range(2):
        source = own_hbm.at[pl.ds(part * half, half)]
        for side in (1, -1):
            send_along(side, 0, me, part, source)
        send_x(me, part, source)
        send_y(me, part, source)
        send_core(me, part, source)

    for load in loads[:4]:
        load.wait()

    @pl.loop(0, docs)
    def _(doc):
        tokens = pl.ds(pl.multiple_of(doc * length, length), length)
        token = lax.broadcasted_iota(jnp.int32, (length, grads.shape[1]), 0)
        valid = (token < lengths[doc]).astype(jnp.float32)
        grads[tokens, :] = (grads[tokens, :].astype(jnp.float32) * valid).astype(jnp.bfloat16)
        reduced_in = jnp.dot(
            act[tokens, :], basis_in[...], preferred_element_type=jnp.float32
        ).astype(jnp.bfloat16)
        reduced_out = jnp.dot(grads[tokens, :], basis_out[...], preferred_element_type=jnp.float32)
        both = jnp.concatenate([reduced_out, reduced_out], axis=1).astype(jnp.bfloat16)
        gram[...] = lax.dot_general(
            reduced_in, both, (((0,), (0,)), ((), ())), preferred_element_type=jnp.float32
        )
        even = gram[pl.ds(0, per_doc, stride=2), :]
        odd = gram[pl.ds(1, per_doc, stride=2), :]
        lane = lax.broadcasted_iota(jnp.int32, (per_doc, 2 * rank), 1)
        projected[pl.ds(pl.multiple_of(me * packed + doc * per_doc, per_doc), per_doc), :] = (
            jnp.where(lane < rank, even, odd).astype(jnp.bfloat16)
        )

    for side in (1, -1):
        send_along(side, 0, me, 2)
    send_x(me, 2)
    send_y(me, 2)
    send_core(me, 2)
    loads[4].wait()
    loads[5].wait()

    def pass_on(step):
        for part in range(PARTS):
            for side in (1, -1):
                @pl.when(exists(side, step))
                def _(side=side):
                    shard = index(at(side, step), y, x, core)
                    arrived(shard, part)
                    send_along(side, step, shard, part)
                    send_x(shard, part)
                    send_y(shard, part)
                    send_core(shard, part)

                if plane:
                    @pl.when(exists(side, step - 1))
                    def _(side=side):
                        level = at(side, step - 1)
                        shard = index(level, y, 1 - x, core)
                        arrived(shard, part)
                        if part == 1:
                            send_y(shard, part)
                        send_core(shard, part)
                        shard = index(level, 1 - y, x, core)
                        arrived(shard, part)
                        if part != 1:
                            send_x(shard, part)
                        send_core(shard, part)

                    @pl.when(exists(side, step - 2))
                    def _(side=side):
                        shard = index(at(side, step - 2), 1 - y, 1 - x, core)
                        arrived(shard, part)
                        send_core(shard, part)

    def multiply(chip):
        for part in range(2):
            arrived(chip * 2 + 1 - core, part)
        block = weight[pl.ds(pl.multiple_of(chip * 2 * rows, 2 * rows), 2 * rows), :]
        columns = pl.ds(pl.multiple_of(chip * 2 * rows, 2 * rows), 2 * rows)
        staged[:, columns] = lax.dot_general(
            grads[...], block, (((1,), (1,)), ((), ())), preferred_element_type=jnp.float32
        ).astype(jnp.bfloat16)
        pltpu.make_async_copy(staged.at[:, columns], out_hbm.at[:, columns], out_sem.at[0]).start()

    def work(step):
        @pl.loop(0, 2 * height * width)
        def _(turn):
            column = lax.div(turn, 2)
            turned = lax.rem(turn, 2)
            off_x = lax.rem(column, 2) if plane else 0
            off_y = lax.div(column, 2) if plane else 0
            far = step - 1 - off_x - off_y
            up = exists(1, far) & (turned == 0)
            down = exists(-1, far) & (turned == 1)
            at_x = x + off_x - 2 * x * off_x
            at_y = y + off_y - 2 * y * off_y
            level = at(1 - 2 * turned, far)

            @pl.when(up | down)
            def _():
                multiply((level * height + at_y) * width + at_x)

    last = reach - 1 + (2 if plane else 0)

    @pl.loop(1, last + 1)
    def _(step):
        pass_on(step)
        work(step)

    @pl.loop(0, chips)
    def _(chip):
        arrived(chip * 2 + 1 - core, 2)

    wide[...] = projected[...].astype(jnp.float32)
    for k in range(per_doc):
        flat[:, k * 2 * rank : (k + 1) * 2 * rank] = wide[
            pl.ds(k, 2 * chips * docs, stride=per_doc), :
        ].astype(jnp.bfloat16)
    scores_ref[...] = lax.dot_general(
        queries[...], flat[...], (((1,), (1,)), ((), ())), preferred_element_type=jnp.float32
    )
    work(last + 1)

    for side in (1, -1):
        @pl.loop(0, reach)
        def _(far, side=side):
            @pl.when((exists(side, far) | (far == 0)) & goes_on(side, far))
            def _():
                shard = index(at(side, far), y, x, core)
                for part in range(PARTS):
                    copy(shard, part, sibling, along(side, far, part)).wait_send()

    def all_sent(which, weight_rows, packed_rows):
        for part, ref, size in ((0, weight, weight_rows), (2, projected, packed_rows)):
            whole = ref.at[pl.ds(0, size)]
            pltpu.make_async_copy(whole, whole, link(which, part)).wait()

    if plane:
        all_sent(LINK_X, depth * (rows + half), depth * 2 * packed)
        all_sent(LINK_Y, depth * (rows + half), depth * packed)
    all_sent(LINK_CORE, chips * rows, chips * packed)
    pltpu.make_async_copy(staged, out_hbm, out_sem.at[0]).wait()


def per_device(dims, wrap, activations, out_grads, value_weight, basis_in, basis_out, doc_lengths, queries):
    docs, length, model = activations.shape
    tokens = docs * length
    inner = out_grads.shape[2]
    rank = basis_in.shape[1]
    chips = dims[0] * dims[1] * dims[2]
    reach = dims[0] // 2 + 1 if wrap else dims[0]
    all_docs = 2 * chips * docs
    per_doc = rank // 2
    hbm = pl.BlockSpec(memory_space=pl.ANY)
    input_grad, scores = pl.pallas_call(
        functools.partial(kernel, dims, wrap),
        out_shape=(
            jax.ShapeDtypeStruct((tokens, model), jnp.bfloat16),
            jax.ShapeDtypeStruct((queries.shape[0], all_docs), jnp.float32),
        ),
        in_specs=[pl.BlockSpec(memory_space=pltpu.SMEM)] + [hbm] * 6,
        out_specs=(hbm, pl.BlockSpec(memory_space=pltpu.VMEM)),
        scratch_shapes=[
            pltpu.VMEM((model, inner), jnp.bfloat16),
            pltpu.VMEM((all_docs * per_doc, 2 * rank), jnp.bfloat16),
            pltpu.VMEM((tokens, model), jnp.bfloat16),
            pltpu.VMEM((tokens, inner), jnp.bfloat16),
            pltpu.VMEM((model, rank), jnp.bfloat16),
            pltpu.VMEM((inner, rank), jnp.bfloat16),
            pltpu.VMEM(queries.shape, jnp.bfloat16),
            pltpu.VMEM((tokens, model), jnp.bfloat16),
            pltpu.VMEM((rank, 2 * rank), jnp.float32),
            pltpu.VMEM((all_docs * per_doc, 2 * rank), jnp.float32),
            pltpu.VMEM((all_docs, rank * rank), jnp.bfloat16),
            pltpu.SemaphoreType.DMA((6,)),
            pltpu.SemaphoreType.DMA((2 * chips * PARTS,)),
            pltpu.SemaphoreType.DMA((2 * reach * PARTS,)),
            pltpu.SemaphoreType.DMA((6,)),
            pltpu.SemaphoreType.DMA((1,)),
        ],
        compiler_params=pltpu.CompilerParams(
            collective_id=0, has_side_effects=True, vmem_limit_bytes=40 * 1024 * 1024
        ),
        cost_estimate=pl.CostEstimate(
            flops=2 * tokens * inner * model, bytes_accessed=4 * tokens * model, transcendentals=0
        ),
    )(
        doc_lengths,
        activations.reshape(tokens, model),
        out_grads.reshape(tokens, inner),
        value_weight,
        basis_in,
        basis_out,
        queries,
    )
    return input_grad.reshape(docs, length, model), scores


def solution(mesh):
    placed = (
        P(("group", "shard"), None, None),
        P(("group", "shard"), None, None),
        P("shard", None),
        P(),
        P(),
        P(("group", "shard")),
        P("shard", None),
    )
    shards = mesh.shape["shard"]
    if mesh.shape["group"] == 1 and shards % 8 == 0:
        dims, wrap = (shards // 8, 2, 2), False
    else:
        dims, wrap = (shards // 2, 1, 1), True
    return jax.shard_map(
        functools.partial(per_device, dims, wrap),
        mesh=mesh,
        in_specs=placed,
        out_specs=(P(("group", "shard"), None, None), P("shard", "group")),
        check_vma=False,
    )
```

time: 109 us -> 61.1 us (0.56)
  Pallas kernels: 0 us -> 49 us
  blocking collectives: 45.8 us -> 0 us
  waiting for transfers between devices: 31.1 us -> 0 us
  matrix products: 16.5 us -> 0 us
  between operations: 14 us -> 0.66 us
  local copies, waits for them, and re-layouts: 0.31 us -> 11.2 us
    pallas_call x0 -> x1, Pallas kernels: none -> 49 us  [per_device(): pl.pallas_call(functools.partial(kernel, dims, wrap), out_shape=(jax.Shap...]
    all_gather x1 -> x0, blocking collectives: 45.8 us -> none  [per_device(): lax.all_gather(projected, 'shard', axis=0, tiled=True)]
    all_gather x1 -> x0, waiting for transfers between devices: 30.4 us -> none  [per_device(): lax.all_gather(value_weight, 'shard', axis=0, tiled=True)]
    dot_general x4 -> x0, matrix products: 16.5 us -> none  [the longest x1 9.46 us: per_device(): jnp.einsum('dtk,jk->dtj', out_grads, lax.all_gather(value_weight, 'shard'...]
    unnamed x4 -> x14, local copies, waits for them, and re-layouts: 0.31 us -> 11.2 us
  transfers between devices with their start and end apart: 1 -> 0, of which waited for: 1 -> 0; matrix products, arithmetic and copies ran while one was open for 7% -> 0% of each run, Pallas kernels for 0% -> 0%
where the time goes in v1:
time: 61.1 us; the launch traced here: 60.8 us
  Pallas kernels  49 us (80%)
  local copies, waits for them, and re-layouts  11.2 us (18%)
  between operations  0.66 us (1%)
    pallas_call x1, Pallas kernels, per_device(): pl.pallas_call(functools.partial(kernel, dims, wrap), out_shape=(jax.Shap...  49 us
    unnamed x14, local copies, waits for them, and re-layouts  11.2 us

profile of v1, /device:TPU:0, one launch (start us, length us, event | category | flops | bytes accessed | tf_op | source)
XLA Modules:
  0.0 60.8 jit_solution(11856520235721690387)
XLA Ops:
  0.6 1.1 %copy.10.basis_out_hbm = bf16[1024,64]{1,0:T(8,128)(2,1)S(1)} copy(bf16[1024,64]{0,1:T(8,128)(2,1)} %param.11) | data formatting | bytes 262144 | tf_op args[4]
  1.7 1.5 %copy.9.basis_in_hbm = bf16[4096,64]{1,0:T(8,128)(2,1)S(1)} copy(bf16[4096,64]{0,1:T(8,128)(2,1)} %param.10) | data formatting | bytes 1048576 | tf_op args[3]
  3.2 0.0 copy-start
  3.2 2.2 %copy-done = bf16[2,256,4096]{2,1,0:T(8,128)(2,1)S(1)} copy-done((bf16[2,256,4096]{2,1,0:T(8,128)(2,1)S(1)}, bf16[2,256,4096]{2,1,0:T(8,128)(2,1)}, u32[]{:S(2)}) %copy-start) | copy-done | bytes 4194328
  5.4 0.0 copy-start.1
  5.4 1.2 %copy-done.1 = bf16[2,256,1024]{2,1,0:T(8,128)(2,1)S(1)} copy-done((bf16[2,256,1024]{2,1,0:T(8,128)(2,1)S(1)}, bf16[2,256,1024]{2,1,0:T(8,128)(2,1)}, u32[]{:S(2)}) %copy-start.1) | copy-done | bytes 1048600
  6.7 0.0 copy-start.2
  6.7 0.9 %copy-done.2 = bf16[128,1024]{1,0:T(8,128)(2,1)S(1)} copy-done((bf16[128,1024]{1,0:T(8,128)(2,1)S(1)}, bf16[128,1024]{1,0:T(8,128)(2,1)}, u32[]{:S(2)}) %copy-start.2) | copy-done | bytes 262168
  7.6 0.0 copy-start.3
  7.6 0.9 %copy-done.3 = bf16[32,4096]{1,0:T(8,128)(2,1)S(1)} copy-done((bf16[32,4096]{1,0:T(8,128)(2,1)S(1)}, bf16[32,4096]{1,0:T(8,128)(2,1)}, u32[]{:S(2)}) %copy-start.3) | copy-done | bytes 262168
  8.6 0.0 copy-start.4
  8.6 0.7 %copy-done.4 = s32[2]{0:T(128)S(1)} copy-done((s32[2]{0:T(128)S(1)}, s32[2]{0:T(128)}, u32[]{:S(2)}) %copy-start.4) | copy-done | bytes 32
  9.2 49.0 %shard_map.86 = (bf16[512,4096]{1,0:T(8,128)(2,1)S(1)}, f32[32,64]{1,0:T(8,128)S(1)}) custom-call(s32[2]{0:T(128)S(1)} %copy-done.4, bf16[512,4096]{1,0:T(8,128)(2,1)S(1)} %bitcast.4, bf16[512,1024]{1,0:T(8,128)(2,1)S(1)} %bitcast.5, bf16[128,1024]{1,0:T(8,128)(2,1)S(1)} %copy-done.2, bf16[4096,64]{1,0:T(8,128)(2,1)S(1)} %copy.9.basis_in_hbm, ...), custom_call_target="tpu_custom_call" | custom-call | flops 4294967296 | bytes 8388608 | tf_op jit(solution)/shard_map/pallas_call | solution.py:301
  58.2 2.0 %copy.13 = bf16[2,256,4096]{2,1,0:T(8,128)(2,1)} copy(bf16[2,256,4096]{2,1,0:T(8,128)(2,1)S(1)} %bitcast.3) | data formatting | bytes 8388608
  60.2 0.6 copy.14
Async XLA Ops:
  3.2 2.2 %copy-start = (bf16[2,256,4096]{2,1,0:T(8,128)(2,1)S(1)}, bf16[2,256,4096]{2,1,0:T(8,128)(2,1)}, u32[]{:S(2)}) copy-start(bf16[2,256,4096]{2,1,0:T(8,128)(2,1)} %param.7) | copy-start | bytes 12582916
  5.4 1.2 %copy-start.1 = (bf16[2,256,1024]{2,1,0:T(8,128)(2,1)S(1)}, bf16[2,256,1024]{2,1,0:T(8,128)(2,1)}, u32[]{:S(2)}) copy-start(bf16[2,256,1024]{2,1,0:T(8,128)(2,1)} %param.8) | copy-start | bytes 3145732
  6.7 0.9 %copy-start.2 = (bf16[128,1024]{1,0:T(8,128)(2,1)S(1)}, bf16[128,1024]{1,0:T(8,128)(2,1)}, u32[]{:S(2)}) copy-start(bf16[128,1024]{1,0:T(8,128)(2,1)} %own_hbm.1) | copy-start | bytes 786436
  7.6 0.9 %copy-start.3 = (bf16[32,4096]{1,0:T(8,128)(2,1)S(1)}, bf16[32,4096]{1,0:T(8,128)(2,1)}, u32[]{:S(2)}) copy-start(bf16[32,4096]{1,0:T(8,128)(2,1)} %queries_hbm.1) | copy-start | bytes 786436
  8.6 0.7 %copy-start.4 = (s32[2]{0:T(128)S(1)}, s32[2]{0:T(128)}, u32[]{:S(2)}) copy-start(s32[2]{0:T(128)} %lengths.1) | copy-start | bytes 28

commit v2 on v1

--- a/solution.py
+++ b/solution.py
@@ -11,11 +11,15 @@
 PARTS = 3
 
 
+def times(a, b):
+    return lax.dot_general(a, b, (((1,), (1,)), ((), ())), preferred_element_type=jnp.float32)
+
+
 def kernel(
     dims, wrap, lengths, act_hbm, grads_hbm, own_hbm, basis_in_hbm, basis_out_hbm, queries_hbm,
     out_hbm, scores_ref,
     weight, projected, act, grads, basis_in, basis_out, queries, staged, gram, wide, flat,
-    load_sem, recv_sem, along_sem, link_sem, out_sem,
+    load_sem, recv_sem, along_sem, diagonal_sem, link_sem, out_sem,
 ):
     depth, height, width = dims
     chips = depth * height * width
@@ -28,7 +32,7 @@
     half = rows // 2
     docs = lengths.shape[0]
     length = grads.shape[0] // docs
-    rank = basis_in.shape[1]
+    rank = basis_in.shape[0]
     packed = projected.shape[0] // (2 * chips)
     per_doc = packed // docs
     plane = width > 1
@@ -59,6 +63,16 @@
         if wrap:
             return far + 1 <= (depth // 2 if side > 0 else (depth - 1) // 2)
         return z > 0 if side > 0 else z < depth - 1
+
+    special = depth // 2
+    at_end = (z == 0) | (z == depth - 1)
+
+    def in_plane(far):
+        return (far == 0) | (at_end & (far == special))
+
+    def diagonal_goes_on(side, far):
+        to_end = z - 1 == 0 if side > 0 else z + 1 == depth - 1
+        return goes_on(side, far) & jnp.logical_not(to_end & (far + 1 == special))
 
     def place(shard, part):
         if part == 2:
@@ -89,6 +103,14 @@
         @pl.when(goes_on(side, far))
         def _():
             copy(shard, part, index(at(-side, 1), y, x, core), along(side, far, part), source).start()
+
+    def diagonal(side, far, part):
+        return diagonal_sem.at[((0 if side > 0 else 1) * reach + far) * PARTS + part]
+
+    def send_diagonal(side, far, shard, part):
+        @pl.when(diagonal_goes_on(side, far))
+        def _():
+            copy(shard, part, index(at(-side, 1), y, x, core), diagonal(side, far, part)).start()
 
     def send_x(shard, part, source=None):
         if plane:
@@ -162,10 +184,8 @@
         token = lax.broadcasted_iota(jnp.int32, (length, grads.shape[1]), 0)
         valid = (token < lengths[doc]).astype(jnp.float32)
         grads[tokens, :] = (grads[tokens, :].astype(jnp.float32) * valid).astype(jnp.bfloat16)
-        reduced_in = jnp.dot(
-            act[tokens, :], basis_in[...], preferred_element_type=jnp.float32
-        ).astype(jnp.bfloat16)
-        reduced_out = jnp.dot(grads[tokens, :], basis_out[...], preferred_element_type=jnp.float32)
+        reduced_in = times(act[tokens, :], basis_in[...]).astype(jnp.bfloat16)
+        reduced_out = times(grads[tokens, :], basis_out[...])
         both = jnp.concatenate([reduced_out, reduced_out], axis=1).astype(jnp.bfloat16)
         gram[...] = lax.dot_general(
             reduced_in, both, (((0,), (0,)), ((), ())), preferred_element_type=jnp.float32
@@ -185,51 +205,51 @@
     loads[4].wait()
     loads[5].wait()
 
-    def pass_on(step):
-        for part in range(PARTS):
-            for side in (1, -1):
-                @pl.when(exists(side, step))
+    def pass_on(step, part):
+        for side in (1, -1):
+            @pl.when(exists(side, step))
+            def _(side=side):
+                shard = index(at(side, step), y, x, core)
+                arrived(shard, part)
+                send_along(side, step, shard, part)
+                send_x(shard, part)
+                send_y(shard, part)
+                send_core(shard, part)
+
+            if plane:
+                @pl.when(exists(side, step - 1))
                 def _(side=side):
-                    shard = index(at(side, step), y, x, core)
+                    level = at(side, step - 1)
+                    shard = index(level, y, 1 - x, core)
                     arrived(shard, part)
-                    send_along(side, step, shard, part)
-                    send_x(shard, part)
-                    send_y(shard, part)
+                    if part == 1:
+                        pl.when(in_plane(step - 1))(lambda: send_y(shard, part))
                     send_core(shard, part)
-
-                if plane:
-                    @pl.when(exists(side, step - 1))
-                    def _(side=side):
-                        level = at(side, step - 1)
-                        shard = index(level, y, 1 - x, core)
-                        arrived(shard, part)
-                        if part == 1:
-                            send_y(shard, part)
-                        send_core(shard, part)
-                        shard = index(level, 1 - y, x, core)
-                        arrived(shard, part)
-                        if part != 1:
-                            send_x(shard, part)
-                        send_core(shard, part)
-
-                    @pl.when(exists(side, step - 2))
-                    def _(side=side):
-                        shard = index(at(side, step - 2), 1 - y, 1 - x, core)
-                        arrived(shard, part)
-                        send_core(shard, part)
+                    other = index(level, 1 - y, x, core)
+                    arrived(other, part)
+                    if part != 1:
+                        pl.when(in_plane(step - 1))(lambda: send_x(other, part))
+                    send_core(other, part)
+
+                @pl.when(exists(side, step - 2))
+                def _(side=side):
+                    shard = index(at(side, step - 2), 1 - y, 1 - x, core)
+                    arrived(shard, part)
+                    send_diagonal(side, step - 2, shard, part)
+                    if side > 0:
+                        pl.when(step == 2)(lambda: send_diagonal(-1, 0, shard, part))
+                    send_core(shard, part)
 
     def multiply(chip):
         for part in range(2):
             arrived(chip * 2 + 1 - core, part)
         block = weight[pl.ds(pl.multiple_of(chip * 2 * rows, 2 * rows), 2 * rows), :]
         columns = pl.ds(pl.multiple_of(chip * 2 * rows, 2 * rows), 2 * rows)
-        staged[:, columns] = lax.dot_general(
-            grads[...], block, (((1,), (1,)), ((), ())), preferred_element_type=jnp.float32
-        ).astype(jnp.bfloat16)
+        staged[:, columns] = times(grads[...], block).astype(jnp.bfloat16)
         pltpu.make_async_copy(staged.at[:, columns], out_hbm.at[:, columns], out_sem.at[0]).start()
 
-    def work(step):
-        @pl.loop(0, 2 * height * width)
+    def work(step, first, stop):
+        @pl.loop(2 * first, 2 * stop)
         def _(turn):
             column = lax.div(turn, 2)
             turned = lax.rem(turn, 2)
@@ -247,11 +267,15 @@
                 multiply((level * height + at_y) * width + at_x)
 
     last = reach - 1 + (2 if plane else 0)
+    columns_of = height * width
 
     @pl.loop(1, last + 1)
     def _(step):
-        pass_on(step)
-        work(step)
+        pass_on(step, 0)
+        work(step, 0, columns_of // 2)
+        pass_on(step, 1)
+        pass_on(step, 2)
+        work(step, columns_of // 2, columns_of)
 
     @pl.loop(0, chips)
     def _(chip):
@@ -262,10 +286,8 @@
         flat[:, k * 2 * rank : (k + 1) * 2 * rank] = wide[
             pl.ds(k, 2 * chips * docs, stride=per_doc), :
         ].astype(jnp.bfloat16)
-    scores_ref[...] = lax.dot_general(
-        queries[...], flat[...], (((1,), (1,)), ((), ())), preferred_element_type=jnp.float32
-    )
-    work(last + 1)
+    scores_ref[...] = times(queries[...], flat[...])
+    work(last + 1, 0, columns_of)
 
     for side in (1, -1):
         @pl.loop(0, reach)
@@ -276,14 +298,25 @@
                 for part in range(PARTS):
                     copy(shard, part, sibling, along(side, far, part)).wait_send()
 
+            if plane:
+                @pl.when((exists(side, far) | (far == 0)) & diagonal_goes_on(side, far))
+                def _():
+                    shard = index(at(side, far), 1 - y, 1 - x, core)
+                    for part in range(PARTS):
+                        copy(shard, part, sibling, diagonal(side, far, part)).wait_send()
+
     def all_sent(which, weight_rows, packed_rows):
         for part, ref, size in ((0, weight, weight_rows), (2, projected, packed_rows)):
             whole = ref.at[pl.ds(0, size)]
             pltpu.make_async_copy(whole, whole, link(which, part)).wait()
 
     if plane:
-        all_sent(LINK_X, depth * (rows + half), depth * 2 * packed)
-        all_sent(LINK_Y, depth * (rows + half), depth * packed)
+        for several, extra in ((jnp.logical_not(at_end), 1), (at_end, 2 if depth > 1 else 1)):
+            @pl.when(several)
+            def _(extra=extra):
+                all_sent(LINK_X, depth * rows + extra * half, (depth + extra) * packed)
+                all_sent(LINK_Y, depth * rows + extra * half, depth * packed)
+
     all_sent(LINK_CORE, chips * rows, chips * packed)
     pltpu.make_async_copy(staged, out_hbm, out_sem.at[0]).wait()
 
@@ -297,7 +330,7 @@
     reach = dims[0] // 2 + 1 if wrap else dims[0]
     all_docs = 2 * chips * docs
     per_doc = rank // 2
-    hbm = pl.BlockSpec(memory_space=pl.ANY)
+    hbm = pl.BlockSpec(memory_space=pltpu.HBM)
     input_grad, scores = pl.pallas_call(
         functools.partial(kernel, dims, wrap),
         out_shape=(
@@ -305,14 +338,14 @@
             jax.ShapeDtypeStruct((queries.shape[0], all_docs), jnp.float32),
         ),
         in_specs=[pl.BlockSpec(memory_space=pltpu.SMEM)] + [hbm] * 6,
-        out_specs=(hbm, pl.BlockSpec(memory_space=pltpu.VMEM)),
+        out_specs=(pl.BlockSpec(memory_space=pl.ANY), pl.BlockSpec(memory_space=pltpu.VMEM)),
         scratch_shapes=[
             pltpu.VMEM((model, inner), jnp.bfloat16),
             pltpu.VMEM((all_docs * per_doc, 2 * rank), jnp.bfloat16),
             pltpu.VMEM((tokens, model), jnp.bfloat16),
             pltpu.VMEM((tokens, inner), jnp.bfloat16),
-            pltpu.VMEM((model, rank), jnp.bfloat16),
-            pltpu.VMEM((inner, rank), jnp.bfloat16),
+            pltpu.VMEM((rank, model), jnp.bfloat16),
+            pltpu.VMEM((rank, inner), jnp.bfloat16),
             pltpu.VMEM(queries.shape, jnp.bfloat16),
             pltpu.VMEM((tokens, model), jnp.bfloat16),
             pltpu.VMEM((rank, 2 * rank), jnp.float32),
@@ -321,11 +354,12 @@
             pltpu.SemaphoreType.DMA((6,)),
             pltpu.SemaphoreType.DMA((2 * chips * PARTS,)),
             pltpu.SemaphoreType.DMA((2 * reach * PARTS,)),
+            pltpu.SemaphoreType.DMA((2 * reach * PARTS,)),
             pltpu.SemaphoreType.DMA((6,)),
             pltpu.SemaphoreType.DMA((1,)),
         ],
         compiler_params=pltpu.CompilerParams(
-            collective_id=0, has_side_effects=True, vmem_limit_bytes=40 * 1024 * 1024
+            collective_id=0, has_side_effects=True, vmem_limit_bytes=60 * 1024 * 1024
         ),
         cost_estimate=pl.CostEstimate(
             flops=2 * tokens * inner * model, bytes_accessed=4 * tokens * model, transcendentals=0
@@ -335,8 +369,8 @@
         activations.reshape(tokens, model),
         out_grads.reshape(tokens, inner),
         value_weight,
-        basis_in,
-        basis_out,
+        basis_in.T,
+        basis_out.T,
         queries,
     )
     return input_grad.reshape(docs, length, model), scores

time: 61.1 us -> 53.5 us (0.88)
  local copies, waits for them, and re-layouts: 11.2 us -> 5.31 us
  Pallas kernels: 49 us -> 47.4 us
    unnamed x14 -> x4, local copies, waits for them, and re-layouts: 11.2 us -> 5.31 us
    pallas_call x1, Pallas kernels: 49 us -> 47.4 us  [per_device(): pl.pallas_call(functools.partial(kernel, dims, wrap), out_shape=(jax.Shap...]
where the time goes in v2:
time: 53.5 us; the launch traced here: 53.3 us
  Pallas kernels  47.4 us (89%)
  local copies, waits for them, and re-layouts  5.31 us (10%)
  between operations  0.65 us (1%)
    pallas_call x1, Pallas kernels, per_device(): pl.pallas_call(functools.partial(kernel, dims, wrap), out_shape=(jax.Shap...  47.4 us
    unnamed x4, local copies, waits for them, and re-layouts  5.31 us

profile of v2, /device:TPU:0, one launch (start us, length us, event | category | flops | bytes accessed | tf_op | source)
XLA Modules:
  0.0 53.3 jit_solution(3480293310664478758)
XLA Ops:
  0.6 47.4 %shard_map.86 = (bf16[512,4096]{1,0:T(8,128)(2,1)}, f32[32,64]{1,0:T(8,128)}) custom-call(s32[2]{0:T(128)} %lengths.1, bf16[512,4096]{1,0:T(8,128)(2,1)} %bitcast.6, bf16[512,1024]{1,0:T(8,128)(2,1)} %bitcast.7, bf16[128,1024]{1,0:T(8,128)(2,1)} %own_hbm.1, bf16[64,4096]{1,0:T(8,128)(2,1)} %bitcast.8, bf16[64,1024]{1,0:T(8,128)(2,1)} %bitcast.9, ...), custom_call_target="tpu_custom_call" | custom-call | flops 4294967296 | bytes 8388608 | tf_op jit(solution)/shard_map/pallas_call | solution.py:334
  48.0 0.0 copy-start
  48.0 4.7 %copy.11 = bf16[2,256,4096]{2,1,0:T(8,128)(2,1)} copy(bf16[2,256,4096]{2,1,0:T(8,128)(2,1)} %bitcast.5) | data formatting | bytes 8388608
  52.7 0.0 copy-done
  52.7 0.6 %copy.12 = f32[32,64]{1,0:T(8,128)} copy(f32[32,64]{1,0:T(8,128)S(1)} %copy-done) | data formatting | bytes 16384
Async XLA Ops:
  48.0 4.7 %copy-start = (f32[32,64]{1,0:T(8,128)S(1)}, f32[32,64]{1,0:T(8,128)}, u32[]{:S(2)}) copy-start(f32[32,64]{1,0:T(8,128)} %get-tuple-element.9) | copy-start | bytes 24580

commit v3 on v2

--- a/solution.py
+++ b/solution.py
@@ -8,7 +8,8 @@
 from jax.sharding import PartitionSpec as P
 
 LINK_X, LINK_Y, LINK_CORE = 0, 1, 2
-PARTS = 3
+ROW_PARTS = 2
+PARTS = ROW_PARTS + 1
 
 
 def times(a, b):
@@ -16,10 +17,10 @@
 
 
 def kernel(
-    dims, wrap, lengths, act_hbm, grads_hbm, own_hbm, basis_in_hbm, basis_out_hbm, queries_hbm,
-    out_hbm, scores_ref,
-    weight, projected, act, grads, basis_in, basis_out, queries, staged, gram, wide, flat,
-    load_sem, recv_sem, along_sem, diagonal_sem, link_sem, out_sem,
+    dims, wrap, lengths_hbm, act_hbm, grads_hbm, own_hbm, basis_in_hbm, basis_out_hbm, queries_hbm,
+    out_ref, scores_ref,
+    lengths, weight, projected, act, grads, basis_in, basis_out, queries, gram, wide, flat,
+    load_sem, recv_sem, along_sem, diagonal_sem, link_sem,
 ):
     depth, height, width = dims
     chips = depth * height * width
@@ -30,6 +31,7 @@
     z = lax.div(me, 2 * width * height)
     rows = own_hbm.shape[0]
     half = rows // 2
+    piece = rows // ROW_PARTS
     docs = lengths.shape[0]
     length = grads.shape[0] // docs
     rank = basis_in.shape[0]
@@ -64,7 +66,7 @@
             return far + 1 <= (depth // 2 if side > 0 else (depth - 1) // 2)
         return z > 0 if side > 0 else z < depth - 1
 
-    special = depth // 2
+    special = depth - 1
     at_end = (z == 0) | (z == depth - 1)
 
     def in_plane(far):
@@ -75,9 +77,9 @@
         return goes_on(side, far) & jnp.logical_not(to_end & (far + 1 == special))
 
     def place(shard, part):
-        if part == 2:
+        if part == ROW_PARTS:
             return projected.at[pl.ds(pl.multiple_of(shard * packed, packed), packed)]
-        return weight.at[pl.ds(pl.multiple_of(shard * rows + part * half, half), half)]
+        return weight.at[pl.ds(pl.multiple_of(shard * rows + part * piece, piece), piece)]
 
     def copy(shard, part, to, send_sem, source=None):
         target = place(shard, part)
@@ -91,7 +93,7 @@
         )
 
     def link(which, part):
-        return link_sem.at[which * 2 + (1 if part == 2 else 0)]
+        return link_sem.at[which * 2 + (1 if part == ROW_PARTS else 0)]
 
     def arrived(shard, part):
         copy(shard, part, sibling, link(LINK_CORE, part)).wait_recv()
@@ -124,6 +126,8 @@
         copy(shard, part, sibling, link(LINK_CORE, part), source).start()
 
     own = weight.at[pl.ds(pl.multiple_of(me * rows, rows), rows)]
+    measures = pltpu.make_async_copy(lengths_hbm, lengths, load_sem.at[6])
+    measures.start()
     loads = [
         pltpu.make_async_copy(source, target, load_sem.at[i])
         for i, (source, target) in enumerate(
@@ -167,14 +171,18 @@
             barrier, partners + jnp.where(z + 1 < depth, 1, 0) + jnp.where(z > 0, 1, 0)
         )
 
-    for part in range(2):
-        source = own_hbm.at[pl.ds(part * half, half)]
+    def send_own(part):
+        source = own_hbm.at[pl.ds(part * piece, piece)]
         for side in (1, -1):
             send_along(side, 0, me, part, source)
         send_x(me, part, source)
         send_y(me, part, source)
         send_core(me, part, source)
 
+    for part in range(ROW_PARTS // 2):
+        send_own(part)
+
+    measures.wait()
     for load in loads[:4]:
         load.wait()
 
@@ -197,15 +205,22 @@
             jnp.where(lane < rank, even, odd).astype(jnp.bfloat16)
         )
 
+        @pl.when(doc == 0)
+        def _():
+            for part in range(ROW_PARTS // 2, ROW_PARTS):
+                send_own(part)
+
     for side in (1, -1):
-        send_along(side, 0, me, 2)
-    send_x(me, 2)
-    send_y(me, 2)
-    send_core(me, 2)
+        send_along(side, 0, me, ROW_PARTS)
+    send_x(me, ROW_PARTS)
+    send_y(me, ROW_PARTS)
+    send_core(me, ROW_PARTS)
     loads[4].wait()
     loads[5].wait()
 
     def pass_on(step, part):
+        by_y = ROW_PARTS // 2 <= part < ROW_PARTS
+
         for side in (1, -1):
             @pl.when(exists(side, step))
             def _(side=side):
@@ -222,12 +237,12 @@
                     level = at(side, step - 1)
                     shard = index(level, y, 1 - x, core)
                     arrived(shard, part)
-                    if part == 1:
+                    if by_y:
                         pl.when(in_plane(step - 1))(lambda: send_y(shard, part))
                     send_core(shard, part)
                     other = index(level, 1 - y, x, core)
                     arrived(other, part)
-                    if part != 1:
+                    if not by_y:
                         pl.when(in_plane(step - 1))(lambda: send_x(other, part))
                     send_core(other, part)
 
@@ -241,12 +256,11 @@
                     send_core(shard, part)
 
     def multiply(chip):
-        for part in range(2):
+        for part in range(ROW_PARTS):
             arrived(chip * 2 + 1 - core, part)
         block = weight[pl.ds(pl.multiple_of(chip * 2 * rows, 2 * rows), 2 * rows), :]
         columns = pl.ds(pl.multiple_of(chip * 2 * rows, 2 * rows), 2 * rows)
-        staged[:, columns] = times(grads[...], block).astype(jnp.bfloat16)
-        pltpu.make_async_copy(staged.at[:, columns], out_hbm.at[:, columns], out_sem.at[0]).start()
+        out_ref[:, columns] = times(grads[...], block).astype(jnp.bfloat16)
 
     def work(step, first, stop):
         @pl.loop(2 * first, 2 * stop)
@@ -271,15 +285,16 @@
 
     @pl.loop(1, last + 1)
     def _(step):
-        pass_on(step, 0)
+        for part in range(ROW_PARTS // 2):
+            pass_on(step, part)
         work(step, 0, columns_of // 2)
-        pass_on(step, 1)
-        pass_on(step, 2)
+        for part in range(ROW_PARTS // 2, PARTS):
+            pass_on(step, part)
         work(step, columns_of // 2, columns_of)
 
     @pl.loop(0, chips)
     def _(chip):
-        arrived(chip * 2 + 1 - core, 2)
+        arrived(chip * 2 + 1 - core, ROW_PARTS)
 
     wide[...] = projected[...].astype(jnp.float32)
     for k in range(per_doc):
@@ -306,7 +321,7 @@
                         copy(shard, part, sibling, diagonal(side, far, part)).wait_send()
 
     def all_sent(which, weight_rows, packed_rows):
-        for part, ref, size in ((0, weight, weight_rows), (2, projected, packed_rows)):
+        for part, ref, size in ((0, weight, weight_rows), (ROW_PARTS, projected, packed_rows)):
             whole = ref.at[pl.ds(0, size)]
             pltpu.make_async_copy(whole, whole, link(which, part)).wait()
 
@@ -318,7 +333,6 @@
                 all_sent(LINK_Y, depth * rows + extra * half, depth * packed)
 
     all_sent(LINK_CORE, chips * rows, chips * packed)
-    pltpu.make_async_copy(staged, out_hbm, out_sem.at[0]).wait()
 
 
 def per_device(dims, wrap, activations, out_grads, value_weight, basis_in, basis_out, doc_lengths, queries):
@@ -334,12 +348,13 @@
     input_grad, scores = pl.pallas_call(
         functools.partial(kernel, dims, wrap),
         out_shape=(
-            jax.ShapeDtypeStruct((tokens, model), jnp.bfloat16),
+            pltpu.VMEM((tokens, model), jnp.bfloat16),
             jax.ShapeDtypeStruct((queries.shape[0], all_docs), jnp.float32),
         ),
-        in_specs=[pl.BlockSpec(memory_space=pltpu.SMEM)] + [hbm] * 6,
-        out_specs=(pl.BlockSpec(memory_space=pl.ANY), pl.BlockSpec(memory_space=pltpu.VMEM)),
+        in_specs=[hbm] * 7,
+        out_specs=(pl.BlockSpec(memory_space=pltpu.VMEM), pl.BlockSpec(memory_space=pltpu.VMEM)),
         scratch_shapes=[
+            pltpu.SMEM((docs,), jnp.int32),
             pltpu.VMEM((model, inner), jnp.bfloat16),
             pltpu.VMEM((all_docs * per_doc, 2 * rank), jnp.bfloat16),
             pltpu.VMEM((tokens, model), jnp.bfloat16),
@@ -347,31 +362,34 @@
             pltpu.VMEM((rank, model), jnp.bfloat16),
             pltpu.VMEM((rank, inner), jnp.bfloat16),
             pltpu.VMEM(queries.shape, jnp.bfloat16),
-            pltpu.VMEM((tokens, model), jnp.bfloat16),
             pltpu.VMEM((rank, 2 * rank), jnp.float32),
             pltpu.VMEM((all_docs * per_doc, 2 * rank), jnp.float32),
             pltpu.VMEM((all_docs, rank * rank), jnp.bfloat16),
-            pltpu.SemaphoreType.DMA((6,)),
+            pltpu.SemaphoreType.DMA((7,)),
             pltpu.SemaphoreType.DMA((2 * chips * PARTS,)),
             pltpu.SemaphoreType.DMA((2 * reach * PARTS,)),
             pltpu.SemaphoreType.DMA((2 * reach * PARTS,)),
             pltpu.SemaphoreType.DMA((6,)),
-            pltpu.SemaphoreType.DMA((1,)),
         ],
         compiler_params=pltpu.CompilerParams(
-            collective_id=0, has_side_effects=True, vmem_limit_bytes=60 * 1024 * 1024
+            collective_id=0, has_side_effects=True, vmem_limit_bytes=40 * 1024 * 1024
         ),
         cost_estimate=pl.CostEstimate(
             flops=2 * tokens * inner * model, bytes_accessed=4 * tokens * model, transcendentals=0
         ),
     )(
-        doc_lengths,
-        activations.reshape(tokens, model),
-        out_grads.reshape(tokens, inner),
-        value_weight,
-        basis_in.T,
-        basis_out.T,
-        queries,
+        *(
+            pltpu.with_memory_space_constraint(a, pltpu.HBM)
+            for a in (
+                doc_lengths,
+                activations.reshape(tokens, model),
+                out_grads.reshape(tokens, inner),
+                value_weight,
+                basis_in.T,
+                basis_out.T,
+                queries,
+            )
+        ),
     )
     return input_grad.reshape(docs, length, model), scores
 

time: 53.5 us -> 47.7 us (0.89)
  Pallas kernels: 47.4 us -> 44.3 us
  local copies, waits for them, and re-layouts: 5.31 us -> 2.62 us
    pallas_call x1, Pallas kernels: 47.4 us -> 44.3 us  [per_device(): pl.pallas_call(functools.partial(kernel, dims, wrap), out_shape=(pltpu.VM...]
    unnamed x4 -> x2, local copies, waits for them, and re-layouts: 5.31 us -> 2.62 us
where the time goes in v3:
time: 47.7 us; the launch traced here: 47.6 us
  Pallas kernels  44.3 us (93%)
  local copies, waits for them, and re-layouts  2.62 us (5%)
  between operations  0.64 us (1%)
    pallas_call x1, Pallas kernels, per_device(): pl.pallas_call(functools.partial(kernel, dims, wrap), out_shape=(pltpu.VM...  44.3 us
    unnamed x2, local copies, waits for them, and re-layouts  2.62 us

profile of v3, /device:TPU:0, one launch (start us, length us, event | category | flops | bytes accessed | tf_op | source)
XLA Modules:
  0.0 47.6 jit_solution(11669640748637193324)
XLA Ops:
  0.6 44.3 %shard_map.86 = (bf16[512,4096]{1,0:T(8,128)(2,1)S(1)}, f32[32,64]{1,0:T(8,128)S(1)}) custom-call(s32[2]{0:T(128)} %lengths_hbm.1, bf16[512,4096]{1,0:T(8,128)(2,1)} %bitcast.6, bf16[512,1024]{1,0:T(8,128)(2,1)} %bitcast.7, bf16[128,1024]{1,0:T(8,128)(2,1)} %own_hbm.1, bf16[64,4096]{1,0:T(8,128)(2,1)} %bitcast.8, bf16[64,1024]{1,0:T(8,128)(2,1)} %bitcast.9, ...), custom_call_target="tpu_custom_call" | custom-call | flops 4294967296 | bytes 8388608 | tf_op jit(solution)/shard_map/pallas_call | solution.py:348
  45.0 2.0 %copy.11 = bf16[2,256,4096]{2,1,0:T(8,128)(2,1)} copy(bf16[2,256,4096]{2,1,0:T(8,128)(2,1)S(1)} %bitcast.5) | data formatting | bytes 8388608
  47.0 0.6 %copy.12 = f32[32,64]{1,0:T(8,128)} copy(f32[32,64]{1,0:T(8,128)S(1)} %get-tuple-element.11) | data formatting | bytes 16384

commit v4 on v3

--- a/solution.py
+++ b/solution.py
@@ -72,6 +72,9 @@
     def in_plane(far):
         return (far == 0) | (at_end & (far == special))
 
+    def waits(far):
+        return at_end & (far >= 1) & (far < depth - 1)
+
     def diagonal_goes_on(side, far):
         to_end = z - 1 == 0 if side > 0 else z + 1 == depth - 1
         return goes_on(side, far) & jnp.logical_not(to_end & (far + 1 == special))
@@ -124,6 +127,31 @@
 
     def send_core(shard, part, source=None):
         copy(shard, part, sibling, link(LINK_CORE, part), source).start()
+
+    barrier = pltpu.get_barrier_semaphore()
+
+    def greet(other):
+        pl.semaphore_signal(barrier, inc=1, device_id=device(other), device_id_type=pl.DeviceIdType.MESH)
+
+    greet(sibling)
+    if plane:
+        greet(beside_x)
+        greet(beside_y)
+    partners = 3 if plane else 1
+    if wrap:
+        greet(index(at(1, 1), y, x, core))
+        greet(index(at(-1, 1), y, x, core))
+        expected = partners + 2
+    else:
+        @pl.when(z + 1 < depth)
+        def _():
+            greet(index(z + 1, y, x, core))
+
+        @pl.when(z > 0)
+        def _():
+            greet(index(z - 1, y, x, core))
+
+        expected = partners + jnp.where(z + 1 < depth, 1, 0) + jnp.where(z > 0, 1, 0)
 
     own = weight.at[pl.ds(pl.multiple_of(me * rows, rows), rows)]
     measures = pltpu.make_async_copy(lengths_hbm, lengths, load_sem.at[6])
@@ -144,32 +172,7 @@
     for load in loads:
         load.start()
 
-    barrier = pltpu.get_barrier_semaphore()
-
-    def greet(other):
-        pl.semaphore_signal(barrier, inc=1, device_id=device(other), device_id_type=pl.DeviceIdType.MESH)
-
-    greet(sibling)
-    if plane:
-        greet(beside_x)
-        greet(beside_y)
-    partners = 3 if plane else 1
-    if wrap:
-        greet(index(at(1, 1), y, x, core))
-        greet(index(at(-1, 1), y, x, core))
-        pl.semaphore_wait(barrier, partners + 2)
-    else:
-        @pl.when(z + 1 < depth)
-        def _():
-            greet(index(z + 1, y, x, core))
-
-        @pl.when(z > 0)
-        def _():
-            greet(index(z - 1, y, x, core))
-
-        pl.semaphore_wait(
-            barrier, partners + jnp.where(z + 1 < depth, 1, 0) + jnp.where(z > 0, 1, 0)
-        )
+    pl.semaphore_wait(barrier, expected)
 
     def send_own(part):
         source = own_hbm.at[pl.ds(part * piece, piece)]
@@ -246,13 +249,19 @@
                         pl.when(in_plane(step - 1))(lambda: send_x(other, part))
                     send_core(other, part)
 
-                @pl.when(exists(side, step - 2))
+                @pl.when(exists(side, step - 2) & jnp.logical_not(waits(step - 2)))
                 def _(side=side):
                     shard = index(at(side, step - 2), 1 - y, 1 - x, core)
                     arrived(shard, part)
                     send_diagonal(side, step - 2, shard, part)
                     if side > 0:
                         pl.when(step == 2)(lambda: send_diagonal(-1, 0, shard, part))
+                    send_core(shard, part)
+
+                @pl.when(exists(side, step - 3) & waits(step - 3))
+                def _(side=side):
+                    shard = index(at(side, step - 3), 1 - y, 1 - x, core)
+                    arrived(shard, part)
                     send_core(shard, part)
 
     def multiply(chip):

time: 47.7 us -> 45.6 us (0.956); the launches traced: 47.6 us -> 44.9 us
  Pallas kernels: 44.3 us -> 41.6 us
    pallas_call x1, Pallas kernels: 44.3 us -> 41.6 us  [per_device(): pl.pallas_call(functools.partial(kernel, dims, wrap), out_shape=(pltpu.VM...]
where the time goes in v4:
time: 45.6 us; the launch traced here: 44.9 us
  Pallas kernels  41.6 us (91%)
  local copies, waits for them, and re-layouts  2.62 us (6%)
  between operations  0.64 us (1%)
    pallas_call x1, Pallas kernels, per_device(): pl.pallas_call(functools.partial(kernel, dims, wrap), out_shape=(pltpu.VM...  41.6 us
    unnamed x2, local copies, waits for them, and re-layouts  2.62 us

profile of v4, /device:TPU:0, one launch (start us, length us, event | category | flops | bytes accessed | tf_op | source)
XLA Modules:
  0.0 44.9 jit_solution(18177934417992957031)
XLA Ops:
  0.6 41.6 %shard_map.86 = (bf16[512,4096]{1,0:T(8,128)(2,1)S(1)}, f32[32,64]{1,0:T(8,128)S(1)}) custom-call(s32[2]{0:T(128)} %lengths_hbm.1, bf16[512,4096]{1,0:T(8,128)(2,1)} %bitcast.6, bf16[512,1024]{1,0:T(8,128)(2,1)} %bitcast.7, bf16[128,1024]{1,0:T(8,128)(2,1)} %own_hbm.1, bf16[64,4096]{1,0:T(8,128)(2,1)} %bitcast.8, bf16[64,1024]{1,0:T(8,128)(2,1)} %bitcast.9, ...), custom_call_target="tpu_custom_call" | custom-call | flops 4294967296 | bytes 8388608 | tf_op jit(solution)/shard_map/pallas_call | solution.py:357
  42.3 2.0 %copy.11 = bf16[2,256,4096]{2,1,0:T(8,128)(2,1)} copy(bf16[2,256,4096]{2,1,0:T(8,128)(2,1)S(1)} %bitcast.5) | data formatting | bytes 8388608
  44.3 0.6 %copy.12 = f32[32,64]{1,0:T(8,128)} copy(f32[32,64]{1,0:T(8,128)S(1)} %get-tuple-element.11) | data formatting | bytes 16384
